TPU v7x, 512 devices: a whole 4x4x16 slice. The times are simulated.
512 devices in a mesh: space: 32 (over z, core), mode: 16 (over y, x).
Axes of the slice: x: 4, y: 4, z: 16, core: 2. Of those that a mesh axis runs over, the one named last changes fastest.
Arguments:
- basis: float32 [3, 256, 16, 8, 2048], P(None, 'space', None, None, 'mode'), may hold values from -132 to 132
- mean_flow: float32 [3, 256, 16, 8], P(None, 'space'), may hold values from -3 to 3
- flow_gradient: float32 [3, 3, 256, 16, 8], P(None, None, 'space'), may hold values from -2 to 2
- viscosity: float32 [256, 16, 8], P('space'), may hold values from 0.02 to 0.2
Outputs:
- reduced: float32 [2048, 2048], P('mode', 'space')
- advected: float32 [3, 256, 16, 8, 2048], P(None, 'space', None, None, 'mode')
- r_factor: float32 [2048, 128], P('mode')
All inputs are finite; a program needn't handle non-finite values.
Results may differ from a plain program's by a relative error of at most 0.00074.
Values may be sent and summed in bfloat16 or wider, within the bound.
No kernel may reach another device: no remote copies, remote signals or barrier semaphores. Data moves between devices by JAX's collectives and lax.ppermute only.
A program may use at most 64 MiB of HBM per device.

v0:
```python
import jax
import jax.numpy as jnp
from jax import lax
from jax.sharding import PartitionSpec as P


def extended(cells, sides, width):
    for axis, dim in sides:
        count = lax.axis_size(axis)
        ends = count - 1
        head = lax.slice_in_dim(cells, 0, width, axis=dim)
        tail = lax.slice_in_dim(cells, cells.shape[dim] - width, cells.shape[dim], axis=dim)
        cells = jnp.concatenate(
            [
                lax.ppermute(tail, axis, [(i, (i + 1) % count) for i in range(ends)]),
                cells,
                lax.ppermute(head, axis, [((i + 1) % count, i) for i in range(ends)]),
            ],
            axis=dim,
        )
    return cells


def transport(padded, mean_flow, flow_gradient, viscosity):
    center = padded[:, 1:-1]
    widen_y = jnp.pad(center, ((0, 0), (0, 0), (1, 1), (0, 0), (0, 0)))
    widen_z = jnp.pad(center, ((0, 0), (0, 0), (0, 0), (1, 1), (0, 0)))
    east_side = padded[:, 2:]
    west_side = padded[:, :-2]
    north_side = widen_y[:, :, 2:]
    south_side = widen_y[:, :, :-2]
    upper_side = widen_z[:, :, :, 2:]
    lower_side = widen_z[:, :, :, :-2]
    laplacian = (
        east_side + west_side + north_side + south_side + upper_side + lower_side - 6.0 * center
    )
    advection = 0.5 * (
        mean_flow[0][None, :, :, :, None] * (east_side - west_side)
        + mean_flow[1][None, :, :, :, None] * (north_side - south_side)
        + mean_flow[2][None, :, :, :, None] * (upper_side - lower_side)
    )
    coupling = flow_gradient[:, 0][..., None] * center[0][None]
    coupling = coupling + flow_gradient[:, 1][..., None] * center[1][None]
    coupling = coupling + flow_gradient[:, 2][..., None] * center[2][None]
    return viscosity[None, :, :, :, None] * laplacian - advection - coupling


def apply_inverse(field, lower_factor):
    width = field.shape[4]
    flat_rows = field.reshape(-1, width)
    solved = jax.scipy.linalg.solve_triangular(lower_factor, flat_rows.T, lower=True)
    return solved.T.reshape(field.shape)


def body(basis, mean_flow, flow_gradient, viscosity):
    cells_x = basis.shape[1]
    cells_y = basis.shape[2]
    cells_z = basis.shape[3]
    panel_width = basis.shape[4]
    weight = 1.0 / (3 * cells_x * cells_y * cells_z * lax.axis_size("space"))
    flat_basis = basis.reshape(-1, panel_width)
    gram_local = (
        jnp.dot(
            flat_basis.T,
            flat_basis,
            precision=lax.Precision.HIGHEST,
            preferred_element_type=jnp.float32,
        )
        * weight
    )
    gram = lax.psum(gram_local, "space")
    lower_factor = jnp.linalg.cholesky(gram)
    ortho = apply_inverse(basis, lower_factor)
    padded_ortho = extended(ortho, (("space", 1),), 1)
    advected = transport(padded_ortho, mean_flow, flow_gradient, viscosity)
    rounded_images = advected.astype(jnp.bfloat16)
    rounded_rows = ortho.astype(jnp.bfloat16).reshape(-1, panel_width)
    panel_piece = lax.all_gather(rounded_images, "mode", axis=4, tiled=True)
    piece_rows = panel_piece.reshape(-1, panel_piece.shape[4])
    strip = (
        jnp.einsum("ra,rk->ak", rounded_rows, piece_rows, preferred_element_type=jnp.float32)
        * weight
    )
    reduced = lax.psum_scatter(strip, "space", scatter_dimension=1, tiled=True)
    return (reduced, advected, lower_factor.T)


def solution(mesh):
    placed = (
        P(None, "space", None, None, "mode"),
        P(None, "space", None, None),
        P(None, None, "space", None, None),
        P("space", None, None),
    )
    return jax.shard_map(
        body,
        mesh=mesh,
        in_specs=placed,
        out_specs=(P("mode", "space"), P(None, "space", None, None, "mode"), P("mode", None)),
        check_vma=False,
    )
```

profile of v0, /device:TPU:2, one launch (start us, length us, event | category | flops | bytes accessed | tf_op | source)
XLA Modules:
  0.0 491.2 jit_solution(15039007794072252386)
XLA Ops:
  7.2 0.0 copy-start
  7.2 0.0 copy-start.5
  7.2 0.0 copy-start.6
  7.2 0.0 all-reduce.4.cloned.1.call-start
  7.2 1.3 copy-done
  8.6 3.3 fusion.8
  11.8 0.0 all-reduce.4.cloned.1.call-update
  11.9 0.0 all-gather.2.cloned.1.call-start
  11.9 0.0 copy-done.5
  12.0 0.0 copy-done.6
  12.0 0.6 slice_bitcast_fusion.5
  12.6 186.8 %all-reduce.4.cloned.1.call-done = f32[128,128]{0,1:T(8,128)} async-done(((f32[128,128]{0,1:T(8,128)}), f32[128,128]{0,1:T(8,128)}) %all-reduce.4.cloned.1.call-update) | async-done | bytes 65552 | tf_op jit(solution)/shard_map/psum | solution.py:71
  199.4 0.9 copy.27
  200.3 0.9 fusion.11
  201.2 11.7 %cholesky.16 = f32[128,128]{1,0:T(8,128)S(1)} custom-call(f32[128,128]{1,0:T(8,128)S(1)} %fusion.11), custom_call_target="Cholesky" | custom-call | tf_op jit(solution)/shard_map/jit(cholesky)/cholesky | solution.py:72
  212.9 0.6 compare_reduce_fusion
  213.5 0.7 fusion.12
  214.2 10.4 %custom-call.7 = f32[1,128,128]{1,2,0:T(8,128)} custom-call(f32[1,128,128]{2,1,0:T(8,128)S(1)} %get-tuple-element.23), custom_call_target="InvertDiagBlocksLowerTriangular" | custom-call | tf_op jit(solution)/shard_map/jit(_solve_triangular)/triangular_solve | solution.py:51
  224.7 2.3 convolution_bitcast_fusion
  227.0 1.6 copy.28
  228.6 1.7 copy.30
  230.3 0.0 copy-start.1
  230.3 0.8 fusion.14
  231.1 1.3 collective-permute-start
  232.4 3.7 collective-permute-start.1
  236.1 1.2 fusion.15
  237.3 0.0 copy-done.1
  237.3 0.0 copy-start.4
  237.3 1.3 copy.36
  238.6 0.9 copy.37
  239.5 0.0 copy-done.4
  239.5 1.0 copy.40
  240.5 2.1 copy.41
  242.6 2.1 copy.38
  244.7 1.1 copy.39
  245.8 0.0 collective-permute-done
  245.8 0.0 collective-permute-done.1
  245.8 0.0 copy-done.2
  245.8 4.9 %fusion.13 = (bf16[3,8,16,8,128]{4,2,3,1,0:T(8,128)(2,1)}, f32[3,8,16,8,128]{4,2,3,1,0:T(8,128)}) fusion(f32[8,16,8,128]{3,1,2,0:T(8,128)} %copy.41, f32[3,8,16,8]{2,3,1,0:T(8,128)S(1)} %get-tuple-element.17, f32[8,16,8,128]{3,1,2,0:T(8,128)S(1)} %copy.39, f32[3,8,16,8]{2,3,1,0:T(8,128)S(1)} %get-tuple-element.18, f32[8,16,8,128]{3,1,2,0:T(8,128)} %copy.37, ...), kind=kLoop, calls=%fused_computation.31 | loop fusion | flops 10616832 | bytes 5951488 | tf_op jit(solution)/shard_map/convert_element_type | solution.py:76
  250.8 0.0 all-gather.2.cloned.1.call-update
  250.8 0.0 reduce-scatter.2.cloned.1.call-start
  250.9 110.3 %all-gather.2.cloned.1.call-done = bf16[3,8,16,8,2048]{4,2,3,1,0:T(8,128)(2,1)} async-done(((bf16[3,8,16,8,128]{4,2,3,1,0:T(8,128)(2,1)}), bf16[3,8,16,8,2048]{4,2,3,1,0:T(8,128)(2,1)}) %all-gather.2.cloned.1.call-update) | async-done | bytes 12582928 | tf_op jit(solution)/shard_map/all_gather | solution.py:78
  361.1 15.4 %fusion.5 = f32[128,2048]{0,1:T(8,128)} fusion(bf16[3,8,16,8,2048]{4,2,3,1,0:T(8,128)(2,1)} %all-gather.2.cloned.1.call-done, f32[3,8,16,8,128]{4,3,2,1,0:T(8,128)} %bitcast.45), kind=kOutput, calls=%fused_computation.6 | convolution fusion | flops 1611268096 | bytes 15204352 | tf_op jit(solution)/shard_map/ra,rk->ak/dot_general | solution.py:81
  376.6 0.0 reduce-scatter.2.cloned.1.call-update
  376.6 0.7 copy.44
  377.3 0.0 copy-done.3
  377.3 1.7 copy.43
  379.1 105.6 %reduce-scatter.2.cloned.1.call-done = f32[128,64]{0,1:T(8,128)} async-done(((f32[128,2048]{0,1:T(8,128)}), f32[128,64]{0,1:T(8,128)}) %reduce-scatter.2.cloned.1.call-update) | async-done | bytes 32784 | tf_op jit(solution)/shard_map/reduce_scatter | solution.py:84
  (4 shorter events, 0.1 us)
Async XLA Ops:
  7.2 1.4 copy-start
  7.2 4.7 copy-start.5
  7.2 4.8 copy-start.6
  7.2 192.2 %all-reduce.4.cloned.1.call-start = ((), (), s32[]{:S(2)}) async-start(), calls=%async_computation.1 | async-start | bytes 131072 | tf_op jit(solution)/shard_map/psum | solution.py:71
  11.9 349.3 %all-gather.2.cloned.1.call-start = ((), (), s32[]{:S(2)}) async-start(), calls=%async_computation.2 | async-start | bytes 13369344 | tf_op jit(solution)/shard_map/all_gather | solution.py:78
  230.3 7.0 %copy-start.1 = (f32[3,8,16,8,128]{4,2,3,1,0:T(8,128)}, f32[3,8,16,8,128]{4,2,3,1,0:T(8,128)S(1)}, u32[]{:S(2)}) copy-start(f32[3,8,16,8,128]{4,2,3,1,0:T(8,128)S(1)} %copy.30) | copy-start | bytes 4718596
  231.1 14.7 %collective-permute-start = (f32[3,1,16,8,128]{4,2,3,1,0:T(8,128)}, f32[3,1,16,8,128]{4,2,3,1,0:T(8,128)}, u32[]{:S(2)}, u32[]{:S(2)}) collective-permute-start(f32[3,1,16,8,128]{4,2,3,1,0:T(8,128)} %get-tuple-element.11), channel_id=1, source_target_pairs={{16,0},{32,16},{48,32},{64,48},{80,64},{96,80},{112,96},{128,112},... | collective-permute-start | bytes 589832 | tf_op jit(solution)/shard_map/ppermute | solution.py:17
  232.4 13.4 %collective-permute-start.1 = (f32[3,1,16,8,128]{4,2,3,1,0:T(8,128)}, f32[3,1,16,8,128]{4,2,3,1,0:T(8,128)}, u32[]{:S(2)}, u32[]{:S(2)}) collective-permute-start(f32[3,1,16,8,128]{4,2,3,1,0:T(8,128)} %get-tuple-element.12), channel_id=1, source_target_pairs={{0,16},{16,32},{32,48},{48,64},{64,80},{80,96},{96,112},{112,128},... | collective-permute-start | bytes 589832 | tf_op jit(solution)/shard_map/ppermute | solution.py:15
  237.3 2.2 copy-start.4
  240.5 5.3 %copy-start.2 = (f32[3,8,16,8,128]{4,2,3,1,0:T(8,128)S(1)}, f32[3,8,16,8,128]{4,2,3,1,0:T(8,128)}, u32[]{:S(2)}) copy-start(f32[3,8,16,8,128]{4,2,3,1,0:T(8,128)} %copy-done.1) | copy-start | bytes 4718596
  250.8 233.9 %reduce-scatter.2.cloned.1.call-start = ((), (), s32[]{:S(2)}) async-start(), calls=%async_computation.3 | async-start | bytes 1081344 | tf_op jit(solution)/shard_map/reduce_scatter | solution.py:84
  361.1 16.2 %copy-start.3 = (f32[3,8,16,8,128]{4,2,3,1,0:T(8,128)S(1)}, f32[3,8,16,8,128]{4,2,3,1,0:T(8,128)}, u32[]{:S(2)}) copy-start(f32[3,8,16,8,128]{4,2,3,1,0:T(8,128)} %get-tuple-element.10) | copy-start | bytes 4718596
Sparse Core Ops, SparseCore 0:
  12.0 187.3 all-reduce.3
  250.9 110.1 all-gather.1
  376.7 107.9 reduce-scatter.1
where the time goes:
time: 492 us; the launch traced here: 491 us
  waiting for transfers between devices  403 us (82%)
  other arithmetic  29.3 us (6%)
  matrix products  21 us (4%)
  local copies, waits for them, and re-layouts  19.2 us (4%)
  between operations  13.9 us (3%)
  starting transfers between devices  5.11 us (1%)
    psum x1, waiting for transfers between devices, body(): gram = lax.psum(gram_local, 'space')  187 us
    all_gather x1, waiting for transfers between devices, body(): panel_piece = lax.all_gather(rounded_images, 'mode', axis=4, tiled=True)  110 us
    reduce_scatter x1, waiting for transfers between devices, body(): reduced = lax.psum_scatter(strip, 'space', scatter_dimension=1, tiled=True)  106 us
    dot_general x1, matrix products, body(): jnp.einsum('ra,rk->ak', rounded_rows, piece_rows, preferred_element_type=...  15.4 us
    another operation x3, other arithmetic, body(): lower_factor = jnp.linalg.cholesky(gram)  12.4 us
    another operation x1, other arithmetic, apply_inverse(): jax.scipy.linalg.solve_triangular(lower_factor, flat_rows.T, lower=True)  10.4 us
  transfers between devices with their start and end apart: 5, of which 3 were waited for; matrix products, arithmetic and copies ran while one was open for 3% of the time, Pallas kernels for 0%

commit v1 on v0

--- a/solution.py
+++ b/solution.py
@@ -68,7 +68,9 @@
         )
         * weight
     )
-    gram = lax.psum(gram_local, "space")
+    gram = gram_local
+    for hop in (1, 2, 4, 8, 16):
+        gram = gram + lax.ppermute(gram, "space", [(dev, dev ^ hop) for dev in range(32)])
     lower_factor = jnp.linalg.cholesky(gram)
     ortho = apply_inverse(basis, lower_factor)
     padded_ortho = extended(ortho, (("space", 1),), 1)

time: 492 us -> 355 us (0.72)
  waiting for transfers between devices: 403 us -> 234 us
  starting transfers between devices: 5.11 us -> 38.9 us
    psum x1 -> x0, waiting for transfers between devices: 187 us -> none  [body(): gram = lax.psum(gram_local, 'space')]
    ppermute x0 -> x5, starting transfers between devices: none -> 33.8 us  [body(): lax.ppermute(gram, 'space', [(dev, dev ^ hop) for dev in range(32)])]
    ppermute x0 -> x5, waiting for transfers between devices: none -> 14 us  [body(): lax.ppermute(gram, 'space', [(dev, dev ^ hop) for dev in range(32)])]
  transfers between devices with their start and end apart: 5 -> 9, of which waited for: 3 -> 7; matrix products, arithmetic and copies ran while one was open for 3% -> 4% of each run, Pallas kernels for 0% -> 0%
where the time goes in v1:
time: 355 us; the launch traced here: 354 us
  waiting for transfers between devices  234 us (66%)
  starting transfers between devices  38.9 us (11%)
  other arithmetic  28.5 us (8%)
  matrix products  20.4 us (6%)
  local copies, waits for them, and re-layouts  18.3 us (5%)
  between operations  14.2 us (4%)
    all_gather x1, waiting for transfers between devices, body(): panel_piece = lax.all_gather(rounded_images, 'mode', axis=4, tiled=True)  114 us
    reduce_scatter x1, waiting for transfers between devices, body(): reduced = lax.psum_scatter(strip, 'space', scatter_dimension=1, tiled=True)  106 us
    ppermute x5, starting transfers between devices, body(): lax.ppermute(gram, 'space', [(dev, dev ^ hop) for dev in range(32)])  33.8 us
    dot_general x1, matrix products, body(): jnp.einsum('ra,rk->ak', rounded_rows, piece_rows, preferred_element_type=...  15.4 us
    ppermute x5, waiting for transfers between devices, body(): lax.ppermute(gram, 'space', [(dev, dev ^ hop) for dev in range(32)])  14 us
    another operation x3, other arithmetic, body(): lower_factor = jnp.linalg.cholesky(gram)  12.4 us
    another operation x1, other arithmetic, apply_inverse(): jax.scipy.linalg.solve_triangular(lower_factor, flat_rows.T, lower=True)  10.4 us
  transfers between devices with their start and end apart: 9, of which 7 were waited for; matrix products, arithmetic and copies ran while one was open for 4% of the time, Pallas kernels for 0%

profile of v1, /device:TPU:2, one launch (start us, length us, event | category | flops | bytes accessed | tf_op | source)
XLA Modules:
  0.0 354.2 jit_solution(15361587352545713712)
XLA Ops:
  7.2 0.0 copy-start
  7.2 0.0 copy-start.5
  7.2 0.0 copy-start.6
  7.2 0.0 all-gather.2.cloned.1.call-start
  7.2 1.3 copy-done
  8.6 2.6 fusion.8
  11.2 1.9 collective-permute-start
  13.1 1.2 collective-permute-done
  14.4 3.8 %collective-permute-start.1 = (f32[128,128]{0,1:T(8,128)S(1)}, f32[128,128]{0,1:T(8,128)S(1)}, u32[]{:S(2)}, u32[]{:S(2)}) collective-permute-start(f32[128,128]{0,1:T(8,128)S(1)} %add.60), channel_id=1, source_target_pairs={{0,32},{16,48},{32,0},{48,16},{64,96},{80,112},{96,64},{112,80},{1... | collective-permute-start | bytes 196616 | tf_op jit(solution)/shard_map/ppermute | solution.py:73
  18.2 2.4 collective-permute-done.1
  20.6 5.2 %collective-permute-start.2 = (f32[128,128]{0,1:T(8,128)S(1)}, f32[128,128]{0,1:T(8,128)S(1)}, u32[]{:S(2)}, u32[]{:S(2)}) collective-permute-start(f32[128,128]{0,1:T(8,128)S(1)} %add.61), channel_id=1, source_target_pairs={{0,64},{16,80},{32,96},{48,112},{64,0},{80,16},{96,32},{112,48},{1... | collective-permute-start | bytes 196616 | tf_op jit(solution)/shard_map/ppermute | solution.py:73
  25.8 2.5 collective-permute-done.2
  28.4 9.1 %collective-permute-start.3 = (f32[128,128]{0,1:T(8,128)S(1)}, f32[128,128]{0,1:T(8,128)S(1)}, u32[]{:S(2)}, u32[]{:S(2)}) collective-permute-start(f32[128,128]{0,1:T(8,128)S(1)} %add.62), channel_id=1, source_target_pairs={{0,128},{16,144},{32,160},{48,176},{64,192},{80,208},{96,224},{112... | collective-permute-start | bytes 196616 | tf_op jit(solution)/shard_map/ppermute | solution.py:73
  37.5 4.8 %collective-permute-done.3 = f32[128,128]{0,1:T(8,128)S(1)} collective-permute-done((f32[128,128]{0,1:T(8,128)S(1)}, f32[128,128]{0,1:T(8,128)S(1)}, u32[]{:S(2)}, u32[]{:S(2)}) %collective-permute-start.3) | collective-permute-done | bytes 65568 | tf_op jit(solution)/shard_map/ppermute | solution.py:73
  42.4 13.8 %collective-permute-start.4 = (f32[128,128]{0,1:T(8,128)S(1)}, f32[128,128]{0,1:T(8,128)S(1)}, u32[]{:S(2)}, u32[]{:S(2)}) collective-permute-start(f32[128,128]{0,1:T(8,128)S(1)} %add.63), channel_id=1, source_target_pairs={{0,256},{16,272},{32,288},{48,304},{64,320},{80,336},{96,352},{112... | collective-permute-start | bytes 196616 | tf_op jit(solution)/shard_map/ppermute | solution.py:73
  56.1 0.6 slice_bitcast_fusion.5
  56.8 3.0 collective-permute-done.4
  59.8 0.1 copy.27
  59.9 11.7 %cholesky.16 = f32[128,128]{1,0:T(8,128)S(1)} custom-call(f32[128,128]{1,0:T(8,128)S(1)} %fusion.11), custom_call_target="Cholesky" | custom-call | tf_op jit(solution)/shard_map/jit(cholesky)/cholesky | solution.py:74
  71.6 0.6 compare_reduce_fusion
  72.3 0.7 fusion.12
  72.9 10.4 %custom-call.7 = f32[1,128,128]{1,2,0:T(8,128)} custom-call(f32[1,128,128]{2,1,0:T(8,128)S(1)} %get-tuple-element.23), custom_call_target="InvertDiagBlocksLowerTriangular" | custom-call | tf_op jit(solution)/shard_map/jit(_solve_triangular)/triangular_solve | solution.py:51
  83.4 2.3 convolution_bitcast_fusion
  85.7 1.6 copy.28
  87.3 1.7 copy.30
  89.0 0.8 fusion.14
  89.9 1.3 collective-permute-start.5
  91.2 3.7 %collective-permute-start.6 = (f32[3,1,16,8,128]{4,2,3,1,0:T(8,128)}, f32[3,1,16,8,128]{4,2,3,1,0:T(8,128)}, u32[]{:S(2)}, u32[]{:S(2)}) collective-permute-start(f32[3,1,16,8,128]{4,2,3,1,0:T(8,128)} %get-tuple-element.12), channel_id=1, source_target_pairs={{0,16},{16,32},{32,48},{48,64},{64,80},{80,96},{96,112},{112,128},... | collective-permute-start | bytes 589832 | tf_op jit(solution)/shard_map/ppermute | solution.py:15
  94.9 1.2 fusion.15
  96.1 0.0 copy-done.1
  96.1 1.3 copy.36
  97.4 0.9 copy.37
  98.3 0.0 copy-done.4
  98.3 1.0 copy.40
  99.3 2.1 copy.41
  101.4 2.0 copy.38
  103.4 1.1 copy.39
  104.5 0.0 collective-permute-done.5
  104.5 0.0 collective-permute-done.6
  104.6 4.9 %fusion.13 = (bf16[3,8,16,8,128]{4,2,3,1,0:T(8,128)(2,1)}, f32[3,8,16,8,128]{4,2,3,1,0:T(8,128)}) fusion(f32[8,16,8,128]{3,1,2,0:T(8,128)} %copy.41, f32[3,8,16,8]{2,3,1,0:T(8,128)S(1)} %get-tuple-element.17, f32[8,16,8,128]{3,1,2,0:T(8,128)S(1)} %copy.39, f32[3,8,16,8]{2,3,1,0:T(8,128)S(1)} %get-tuple-element.18, f32[8,16,8,128]{3,1,2,0:T(8,128)} %copy.37, ...), kind=kLoop, calls=%fused_computation.31 | loop fusion | flops 10616832 | bytes 5951488 | tf_op jit(solution)/shard_map/convert_element_type | solution.py:78
  109.5 0.0 all-gather.2.cloned.1.call-update
  109.5 0.0 reduce-scatter.2.cloned.1.call-start
  109.6 114.2 %all-gather.2.cloned.1.call-done = bf16[3,8,16,8,2048]{4,2,3,1,0:T(8,128)(2,1)} async-done(((bf16[3,8,16,8,128]{4,2,3,1,0:T(8,128)(2,1)}), bf16[3,8,16,8,2048]{4,2,3,1,0:T(8,128)(2,1)}) %all-gather.2.cloned.1.call-update) | async-done | bytes 12582928 | tf_op jit(solution)/shard_map/all_gather | solution.py:80
  223.8 15.4 %fusion.5 = f32[128,2048]{0,1:T(8,128)} fusion(bf16[3,8,16,8,2048]{4,2,3,1,0:T(8,128)(2,1)} %all-gather.2.cloned.1.call-done, f32[3,8,16,8,128]{4,3,2,1,0:T(8,128)} %bitcast.45), kind=kOutput, calls=%fused_computation.6 | convolution fusion | flops 1611268096 | bytes 15204352 | tf_op jit(solution)/shard_map/ra,rk->ak/dot_general | solution.py:83
  239.2 0.0 reduce-scatter.2.cloned.1.call-update
  239.3 0.7 copy.44
  240.0 1.7 copy.43
  241.7 105.6 %reduce-scatter.2.cloned.1.call-done = f32[128,64]{0,1:T(8,128)} async-done(((f32[128,2048]{0,1:T(8,128)}), f32[128,64]{0,1:T(8,128)}) %reduce-scatter.2.cloned.1.call-update) | async-done | bytes 32784 | tf_op jit(solution)/shard_map/reduce_scatter | solution.py:86
  (16 shorter events, 0.1 us)
Async XLA Ops:
  7.2 1.4 copy-start
  7.2 30.3 %copy-start.5 = (f32[3,3,8,16,8]{3,4,2,1,0:T(8,128)S(1)}, f32[3,3,8,16,8]{3,4,2,1,0:T(8,128)}, u32[]{:S(2)}) copy-start(f32[3,3,8,16,8]{3,4,2,1,0:T(8,128)} %param.6) | copy-start | bytes 110596
  7.2 48.9 %copy-start.6 = (f32[3,8,16,8]{2,3,1,0:T(8,128)S(1)}, f32[3,8,16,8]{2,3,1,0:T(8,128)}, u32[]{:S(2)}) copy-start(f32[3,8,16,8]{2,3,1,0:T(8,128)} %param.5) | copy-start | bytes 36868
  7.2 216.6 %all-gather.2.cloned.1.call-start = ((), (), s32[]{:S(2)}) async-start(), calls=%async_computation.1 | async-start | bytes 13369344 | tf_op jit(solution)/shard_map/all_gather | solution.py:80
  11.2 3.1 collective-permute-start
  14.4 6.2 %collective-permute-start.1 = (f32[128,128]{0,1:T(8,128)S(1)}, f32[128,128]{0,1:T(8,128)S(1)}, u32[]{:S(2)}, u32[]{:S(2)}) collective-permute-start(f32[128,128]{0,1:T(8,128)S(1)} %add.60), channel_id=1, source_target_pairs={{0,32},{16,48},{32,0},{48,16},{64,96},{80,112},{96,64},{112,80},{1... | collective-permute-start | bytes 196616 | tf_op jit(solution)/shard_map/ppermute | solution.py:73
  20.6 7.7 %collective-permute-start.2 = (f32[128,128]{0,1:T(8,128)S(1)}, f32[128,128]{0,1:T(8,128)S(1)}, u32[]{:S(2)}, u32[]{:S(2)}) collective-permute-start(f32[128,128]{0,1:T(8,128)S(1)} %add.61), channel_id=1, source_target_pairs={{0,64},{16,80},{32,96},{48,112},{64,0},{80,16},{96,32},{112,48},{1... | collective-permute-start | bytes 196616 | tf_op jit(solution)/shard_map/ppermute | solution.py:73
  28.4 14.0 %collective-permute-start.3 = (f32[128,128]{0,1:T(8,128)S(1)}, f32[128,128]{0,1:T(8,128)S(1)}, u32[]{:S(2)}, u32[]{:S(2)}) collective-permute-start(f32[128,128]{0,1:T(8,128)S(1)} %add.62), channel_id=1, source_target_pairs={{0,128},{16,144},{32,160},{48,176},{64,192},{80,208},{96,224},{112... | collective-permute-start | bytes 196616 | tf_op jit(solution)/shard_map/ppermute | solution.py:73
  42.4 17.4 %collective-permute-start.4 = (f32[128,128]{0,1:T(8,128)S(1)}, f32[128,128]{0,1:T(8,128)S(1)}, u32[]{:S(2)}, u32[]{:S(2)}) collective-permute-start(f32[128,128]{0,1:T(8,128)S(1)} %add.63), channel_id=1, source_target_pairs={{0,256},{16,272},{32,288},{48,304},{64,320},{80,336},{96,352},{112... | collective-permute-start | bytes 196616 | tf_op jit(solution)/shard_map/ppermute | solution.py:73
  89.0 7.0 %copy-start.1 = (f32[3,8,16,8,128]{4,2,3,1,0:T(8,128)}, f32[3,8,16,8,128]{4,2,3,1,0:T(8,128)S(1)}, u32[]{:S(2)}) copy-start(f32[3,8,16,8,128]{4,2,3,1,0:T(8,128)S(1)} %copy.30) | copy-start | bytes 4718596
  89.9 14.7 %collective-permute-start.5 = (f32[3,1,16,8,128]{4,2,3,1,0:T(8,128)}, f32[3,1,16,8,128]{4,2,3,1,0:T(8,128)}, u32[]{:S(2)}, u32[]{:S(2)}) collective-permute-start(f32[3,1,16,8,128]{4,2,3,1,0:T(8,128)} %get-tuple-element.11), channel_id=1, source_target_pairs={{16,0},{32,16},{48,32},{64,48},{80,64},{96,80},{112,96},{128,112},... | collective-permute-start | bytes 589832 | tf_op jit(solution)/shard_map/ppermute | solution.py:17
  91.2 13.4 %collective-permute-start.6 = (f32[3,1,16,8,128]{4,2,3,1,0:T(8,128)}, f32[3,1,16,8,128]{4,2,3,1,0:T(8,128)}, u32[]{:S(2)}, u32[]{:S(2)}) collective-permute-start(f32[3,1,16,8,128]{4,2,3,1,0:T(8,128)} %get-tuple-element.12), channel_id=1, source_target_pairs={{0,16},{16,32},{32,48},{48,64},{64,80},{80,96},{96,112},{112,128},... | collective-permute-start | bytes 589832 | tf_op jit(solution)/shard_map/ppermute | solution.py:15
  96.1 2.2 copy-start.4
  99.3 5.3 %copy-start.2 = (f32[3,8,16,8,128]{4,2,3,1,0:T(8,128)S(1)}, f32[3,8,16,8,128]{4,2,3,1,0:T(8,128)}, u32[]{:S(2)}) copy-start(f32[3,8,16,8,128]{4,2,3,1,0:T(8,128)} %copy-done.1) | copy-start | bytes 4718596
  109.5 237.8 %reduce-scatter.2.cloned.1.call-start = ((), (), s32[]{:S(2)}) async-start(), calls=%async_computation.2 | async-start | bytes 1081344 | tf_op jit(solution)/shard_map/reduce_scatter | solution.py:86
  223.8 16.2 %copy-start.3 = (f32[3,8,16,8,128]{4,2,3,1,0:T(8,128)S(1)}, f32[3,8,16,8,128]{4,2,3,1,0:T(8,128)}, u32[]{:S(2)}) copy-start(f32[3,8,16,8,128]{4,2,3,1,0:T(8,128)} %get-tuple-element.10) | copy-start | bytes 4718596
Sparse Core Ops, SparseCore 0:
  109.6 114.1 all-gather.1
  239.4 107.9 reduce-scatter.1
